TPU v7x, 256 devices: a whole 4x4x8 slice. The times are simulated.
256 devices in a mesh: dp: 32 (over z_lo, y, core), tensor: 8 (over z_hi, x).
Axes of the slice: x: 4, y: 4, z: 8 (z_hi: 2, z_lo: 4; z = z_hi * 4 + z_lo), core: 2. Of those that a mesh axis runs over, the one named last changes fastest.
Arguments:
- tokens: bfloat16 [512, 8192], P('dp', 'tensor'), may hold values from -6 to 6
- reflectors: float32 [8192, 256], P('tensor'), may hold values from -0.0625 to 0.0625
- gate_weight: bfloat16 [8192, 28672], P('tensor', 'dp'), may hold values from -0.0625 to 0.0625
- up_weight: bfloat16 [8192, 28672], P('tensor', 'dp'), may hold values from -0.0625 to 0.0625
- down_weight: bfloat16 [28672, 8192], P('dp', 'tensor'), may hold values from -0.03125 to 0.03125
- grad_out: bfloat16 [512, 8192], P('dp', 'tensor'), may hold values from -0.059814453 to 0.059814453
Outputs:
- mixed: bfloat16 [512, 8192], P('dp', 'tensor')
- reflector_grad: float32 [8192, 256], P('tensor')
All inputs are finite; a program needn't handle non-finite values.
Results may differ from a plain program's by a relative error of at most 0.0065.
Values may be sent and summed in bfloat16 or wider, within the bound.
A program may use at most 128 MiB of HBM per device.

v0:
```python
import jax
import jax.numpy as jnp
from jax import lax
from jax.sharding import PartitionSpec as P


def activate(pre, width):
    gate = pre[:, :width]
    up = pre[:, width:]
    sigma = jax.nn.sigmoid(gate)
    return (gate * sigma * up).astype(jnp.bfloat16)


def backprop(pre, d_hidden, width):
    gate = pre[:, :width]
    up = pre[:, width:]
    sigma = jax.nn.sigmoid(gate)
    d_gate = (d_hidden * up * sigma * (1.0 + gate * (1.0 - sigma))).astype(jnp.bfloat16)
    d_up = (d_hidden * gate * sigma).astype(jnp.bfloat16)
    return jnp.concatenate([d_gate, d_up], axis=1)


def invert_upper(coupling):
    highest = lax.Precision.HIGHEST
    order = coupling.shape[0]
    diag_vals = jnp.diag(coupling)
    strict = jnp.triu(coupling, 1) / diag_vals[:, None]
    ident = jnp.eye(order, dtype=jnp.float32)
    power = -strict
    result = ident
    for level in range(max(order.bit_length(), 1)):
        result = jnp.dot(result, ident + power, precision=highest)
        power = jnp.dot(power, power, precision=highest)
    return result / diag_vals[None, :]


def body(tokens, reflectors, gate_weight, up_weight, down_weight, grad_out):
    highest = lax.Precision.HIGHEST
    acts = tokens.astype(jnp.float32)
    width = gate_weight.shape[1]
    gram_part = jnp.dot(reflectors.T, reflectors, precision=highest)
    proj_part = jnp.dot(acts, reflectors, precision=highest)
    gram, proj = lax.psum((gram_part, proj_part), "tensor")
    coupling = jnp.triu(gram, 1) + 0.5 * jnp.diag(jnp.diag(gram))
    inverse = invert_upper(coupling)
    coeffs = jnp.dot(proj, inverse, precision=highest)
    reflected = (acts - jnp.dot(coeffs, reflectors.T, precision=highest)).astype(jnp.bfloat16)
    weights = jnp.concatenate([gate_weight, up_weight], axis=1)
    partial_pre = jnp.dot(
        lax.all_gather(reflected, "dp", axis=0, tiled=True),
        weights,
        preferred_element_type=jnp.float32,
    )
    pre_share = lax.psum_scatter(partial_pre, "tensor", scatter_dimension=0, tiled=True)
    hidden_share = activate(pre_share, width)
    hidden_all = lax.all_gather(hidden_share, "tensor", axis=0, tiled=True)
    rows = hidden_all
    mixed = lax.psum_scatter(
        jnp.dot(rows, down_weight, preferred_element_type=jnp.float32),
        "dp",
        scatter_dimension=0,
        tiled=True,
    ).astype(jnp.bfloat16)
    partial_grad = lax.dot_general(
        lax.all_gather(grad_out, "dp", axis=0, tiled=True),
        down_weight,
        (((1,), (1,)), ((), ())),
        preferred_element_type=jnp.float32,
    )
    d_hidden = lax.psum_scatter(partial_grad, "tensor", scatter_dimension=0, tiled=True)
    d_pre_share = backprop(pre_share, d_hidden, width)
    d_pre_all = lax.all_gather(d_pre_share, "tensor", axis=0, tiled=True)
    rows = d_pre_all
    d_reflected = lax.psum_scatter(
        lax.dot_general(
            rows, weights, (((1,), (1,)), ((), ())), preferred_element_type=jnp.float32
        ),
        "dp",
        scatter_dimension=0,
        tiled=True,
    )
    d_coeffs = -lax.psum(jnp.dot(d_reflected, reflectors, precision=highest), "tensor")
    d_proj = jnp.dot(d_coeffs, inverse.T, precision=highest)
    local_grad = -jnp.dot(d_reflected.T, coeffs, precision=highest) + jnp.dot(
        acts.T, d_proj, precision=highest
    )
    local_cross = jnp.dot(coeffs.T, d_proj, precision=highest)
    summed_grad, cross = lax.psum((local_grad, local_cross), "dp")
    d_coupling = -cross
    d_gram = jnp.triu(d_coupling, 1) + 0.5 * jnp.diag(jnp.diag(d_coupling))
    grad = summed_grad + jnp.dot(reflectors, d_gram + d_gram.T, precision=highest)
    return (mixed, grad)


def solution(mesh):
    placed = (
        P("dp", "tensor"),
        P("tensor", None),
        P("tensor", "dp"),
        P("tensor", "dp"),
        P("dp", "tensor"),
        P("dp", "tensor"),
    )
    return jax.shard_map(
        body,
        mesh=mesh,
        in_specs=placed,
        out_specs=(P("dp", "tensor"), P("tensor", None)),
        check_vma=False,
    )
```

profile of v0, /device:TPU:1, one launch (start us, length us, event | category | flops | bytes accessed | tf_op | source)
XLA Modules:
  0.0 1013.5 jit_solution(3853232041427407298)
XLA Ops:
  8.0 0.0 all-reduce.4.cloned.1.call-start
  8.1 4.2 fusion.15
  12.3 0.0 all-gather.6.cloned.1.call-start
  12.4 0.5 all-gather.6.cloned.1.call-update
  12.9 0.0 all-gather.4.cloned.1.call-start
  13.0 0.5 fusion.14
  13.4 49.4 %psum.35 = f32[16,256]{1,0:T(8,128)S(1)} all-reduce(f32[16,256]{1,0:T(8,128)S(1)} %fusion.14), channel_id=1, replica_groups=mesh['dp'=32,'tensor'=8] {'tensor'}, use_global_device_ids=true, to_apply=%region_0.0 | all-reduce | flops 4096 | bytes 32768 | tf_op jit(solution)/shard_map/psum | solution.py:43
  62.8 54.8 %all-reduce.4.cloned.1.call-done = f32[256,256]{1,0:T(8,128)} async-done(((f32[256,256]{1,0:T(8,128)}), f32[256,256]{1,0:T(8,128)}) %all-reduce.4.cloned.1.call-update) | async-done | bytes 262160 | tf_op jit(solution)/shard_map/psum | solution.py:43
  117.7 2.6 gather_fusion
  120.2 1.1 multiply_add_fusion.1
  121.3 2.3 gather_fusion.1
  123.6 0.5 fusion.13
  124.1 0.4 fusion.3
  124.6 0.4 fusion.16
  124.9 0.4 fusion.4
  125.3 0.4 fusion.17
  125.7 0.4 fusion.5
  126.1 0.4 fusion.18
  126.5 0.4 fusion.6
  126.9 0.4 fusion.19
  127.3 0.4 fusion.7
  127.7 0.4 fusion.20
  128.1 0.4 fusion.8
  128.5 0.4 fusion.21
  128.9 0.4 fusion.9
  129.3 0.4 convolution_add_fusion
  129.7 0.4 fusion.10
  130.1 0.4 convolution_divide_fusion
  130.5 0.2 fusion.22
  130.7 1.6 fusion.2
  132.3 0.2 reduce-scatter.9.cloned.1.call-start
  132.6 3.8 fusion.25
  136.4 0.0 reduce-scatter.5.cloned.1.call-start
  136.5 3.1 constant_dynamic-update-slice_fusion.1
  139.6 1.4 constant_dynamic-update-slice_fusion
  141.0 58.3 %all-gather.4.cloned.1.call-done = bf16[512,1024]{1,0:T(8,128)(2,1)} async-done(((bf16[16,1024]{1,0:T(8,128)(2,1)}), bf16[512,1024]{1,0:T(8,128)(2,1)}) %all-gather.4.cloned.1.call-update) | async-done | bytes 1048592 | tf_op jit(solution)/shard_map/all_gather | solution.py:50
  199.3 6.2 fusion.23
  205.5 0.0 all-gather.8.cloned.1.call-start
  205.6 24.9 %reduce-scatter.9.cloned.1.call-done = f32[64,896]{1,0:T(8,128)} async-done(((f32[512,896]{1,0:T(8,128)}), f32[64,896]{1,0:T(8,128)}) %reduce-scatter.9.cloned.1.call-update) | async-done | bytes 229392 | tf_op jit(solution)/shard_map/reduce_scatter | solution.py:70
  230.5 121.6 %reduce-scatter.5.cloned.1.call-done = f32[64,1792]{1,0:T(8,128)} async-done(((f32[512,1792]{1,0:T(8,128)}), f32[64,1792]{1,0:T(8,128)}) %reduce-scatter.5.cloned.1.call-update) | async-done | bytes 458768 | tf_op jit(solution)/shard_map/reduce_scatter | solution.py:54
  352.1 1.3 multiply_convert_fusion.1
  353.3 0.7 pad_maximum_fusion
  354.1 0.0 reduce-scatter.11.cloned.1.call-start
  354.1 69.3 %all-gather.8.cloned.1.call-done = bf16[512,1792]{1,0:T(8,128)(2,1)} async-done(((bf16[64,1792]{1,0:T(8,128)(2,1)}), bf16[512,1792]{1,0:T(8,128)(2,1)}) %all-gather.8.cloned.1.call-update) | async-done | bytes 1835024 | tf_op jit(solution)/shard_map/all_gather | solution.py:72
  423.5 6.1 fusion.26
  429.6 0.0 reduce-scatter.7.cloned.1.call-start
  429.6 41.3 %all_gather.13 = bf16[512,896]{1,0:T(8,128)(2,1)S(1)} all-gather(bf16[64,896]{1,0:T(8,128)(2,1)S(1)} %get-tuple-element.6), channel_id=1, replica_groups=mesh['dp'=32,'tensor'=8] {'tensor'}, dimensions={0}, use_global_device_ids=true | all-gather | bytes 1032192 | tf_op jit(solution)/shard_map/all_gather | solution.py:56
  470.9 2.6 fusion.24
  473.6 0.0 all-reduce.6.cloned.1.call-start
  473.6 96.0 %reduce-scatter.11.cloned.1.call-done = f32[16,1024]{1,0:T(8,128)} async-done(((f32[512,1024]{1,0:T(8,128)}), f32[16,1024]{1,0:T(8,128)}) %reduce-scatter.11.cloned.1.call-update) | async-done | bytes 65552 | tf_op jit(solution)/shard_map/reduce_scatter | solution.py:74
  569.7 1.4 fusion.27
  571.0 46.6 %psum.37 = f32[16,256]{1,0:T(8,128)S(1)} all-reduce(f32[16,256]{1,0:T(8,128)S(1)} %fusion.27), channel_id=1, replica_groups=mesh['dp'=32,'tensor'=8] {'tensor'}, use_global_device_ids=true, to_apply=%region_6.7 | all-reduce | flops 4096 | bytes 32768 | tf_op jit(solution)/shard_map/psum | solution.py:82
  617.6 0.3 fusion.11
  617.9 1.2 fusion.28
  619.1 1.9 convolution_negate_fusion
  621.0 1.6 fusion
  622.6 92.5 %reduce-scatter.7.cloned.1.call-done = f32[16,1024]{1,0:T(8,128)} async-done(((f32[512,1024]{1,0:T(8,128)}), f32[16,1024]{1,0:T(8,128)}) %reduce-scatter.7.cloned.1.call-update) | async-done | bytes 65552 | tf_op jit(solution)/shard_map/reduce_scatter | solution.py:58
  715.0 1.5 convert_element_type.41
  716.5 281.9 %all-reduce.6.cloned.1.call-done = (f32[1024,256]{1,0:T(8,128)}, f32[256,256]{1,0:T(8,128)}) async-done(((f32[1024,256]{1,0:T(8,128)}, f32[256,256]{1,0:T(8,128)}), (f32[1024,256]{1,0:T(8,128)}, f32[256,256]{1,0:T(8,128)})) %all-reduce.6.cloned.1.call-update) | async-done | bytes 1310736 | tf_op jit(solution)/shard_map/psum | solution.py:88
  998.4 1.0 neg.20
  999.4 2.3 gather_fusion.2
  1001.7 1.0 multiply_add_fusion
  1002.8 0.1 copy.12
  1002.9 3.2 fusion.1
  (18 shorter events, 0.2 us)
Async XLA Ops:
  8.0 124.6 %copy-start = (bf16[896,1024]{1,0:T(8,128)(2,1)S(1)}, bf16[896,1024]{1,0:T(8,128)(2,1)}, u32[]{:S(2)}) copy-start(bf16[896,1024]{1,0:T(8,128)(2,1)} %param.10) | copy-start | bytes 5505028
  8.0 5.0 copy-start.1
  8.0 5.0 copy-start.3
  8.0 109.6 %all-reduce.4.cloned.1.call-start = ((), (), s32[]{:S(2)}) async-start(), calls=%async_computation.4 | async-start | bytes 524288 | tf_op jit(solution)/shard_map/psum | solution.py:43
  12.3 120.3 %all-gather.6.cloned.1.call-start = ((), (), s32[]{:S(2)}) async-start(), calls=%async_computation.8 | async-start | bytes 1081344 | tf_op jit(solution)/shard_map/all_gather | solution.py:65
  12.9 186.4 %all-gather.4.cloned.1.call-start = ((), (), s32[]{:S(2)}) async-start(), calls=%async_computation.5 | async-start | bytes 1081344 | tf_op jit(solution)/shard_map/all_gather | solution.py:50
  132.3 98.1 %reduce-scatter.9.cloned.1.call-start = ((), (), s32[]{:S(2)}) async-start(), calls=%async_computation.9 | async-start | bytes 2064384 | tf_op jit(solution)/shard_map/reduce_scatter | solution.py:70
  136.4 215.6 %reduce-scatter.5.cloned.1.call-start = ((), (), s32[]{:S(2)}) async-start(), calls=%async_computation.6 | async-start | bytes 4128768 | tf_op jit(solution)/shard_map/reduce_scatter | solution.py:54
  136.5 3.1 copy-start.2
  205.5 217.9 %all-gather.8.cloned.1.call-start = ((), (), s32[]{:S(2)}) async-start(), calls=%async_computation.10 | async-start | bytes 2064384 | tf_op jit(solution)/shard_map/all_gather | solution.py:72
  354.1 215.6 %reduce-scatter.11.cloned.1.call-start = ((), (), s32[]{:S(2)}) async-start(), calls=%async_computation.11 | async-start | bytes 2162688 | tf_op jit(solution)/shard_map/reduce_scatter | solution.py:74
  429.6 285.5 %reduce-scatter.7.cloned.1.call-start = ((), (), s32[]{:S(2)}) async-start(), calls=%async_computation.7 | async-start | bytes 2162688 | tf_op jit(solution)/shard_map/reduce_scatter | solution.py:58
  473.6 524.8 %all-reduce.6.cloned.1.call-start = ((), (), s32[]{:S(2)}) async-start(), calls=%async_computation.12 | async-start | bytes 2621440 | tf_op jit(solution)/shard_map/psum | solution.py:88
Sparse Core Ops, SparseCore 0:
  12.4 105.1 all-reduce.3
  137.8 92.6 reduce-scatter.8
  235.3 116.6 reduce-scatter.4
  355.1 68.3 all-gather.7
Sparse Core Ops, SparseCore 1:
  14.6 63.4 all-gather.5
  132.4 66.8 all-gather.3
  429.7 139.9 reduce-scatter.10
  572.3 142.6 reduce-scatter.6
  718.3 280.0 all-reduce.5
where the time goes:
time: 1010 us
  waiting for transfers between devices  800 us (79%)
  blocking collectives  137 us (14%)
  matrix products  41.4 us (4%)
  between operations  15.8 us (2%)
  local copies, waits for them, and re-layouts  11.9 us (1%)
    psum x1, waiting for transfers between devices, body(): summed_grad, cross = lax.psum((local_grad, local_cross), 'dp')  282 us
    reduce_scatter x1, waiting for transfers between devices, body(): lax.psum_scatter(partial_pre, 'tensor', scatter_dimension=0, tiled=True)  122 us
    reduce_scatter x1, waiting for transfers between devices, body(): lax.psum_scatter(lax.dot_general(rows, weights, (((1,), (1,)), ((), ())),...  96 us
    reduce_scatter x1, waiting for transfers between devices, body(): lax.psum_scatter(jnp.dot(rows, down_weight, preferred_element_type=jnp.fl...  92.5 us
    all_gather x1, waiting for transfers between devices, body(): d_pre_all = lax.all_gather(d_pre_share, 'tensor', axis=0, tiled=True)  69.3 us
    all_gather x1, waiting for transfers between devices, body(): lax.all_gather(reflected, 'dp', axis=0, tiled=True)  58.3 us
    psum x1, waiting for transfers between devices, body(): gram, proj = lax.psum((gram_part, proj_part), 'tensor')  54.8 us
    psum x1, blocking collectives, body(): gram, proj = lax.psum((gram_part, proj_part), 'tensor')  49.4 us
  transfers between devices with their start and end apart: 9, of which 8 were waited for; matrix products, arithmetic and copies ran while one was open for 4% of the time, Pallas kernels for 0%

commit v1 on v0

v1 whole, which is shorter than its diff:
```python
import functools

import jax
import jax.numpy as jnp
from jax import lax
from jax.experimental import pallas as pl
from jax.experimental.pallas import tpu as pltpu
from jax.sharding import PartitionSpec as P

MESH = pl.DeviceIdType.MESH
BF = jnp.bfloat16
F32 = jnp.float32
HI = lax.Precision.HIGHEST

D, FF, R, TOKENS = 8192, 28672, 256, 512
DB = D // 8
FB = FF // 32
TB = TOKENS // 32
GB = R // 32
DO = DB // 32
SEMS = 144


def nn(a, b):
    return jnp.dot(a, b, preferred_element_type=F32)


def nt(a, b):
    return lax.dot_general(a, b, (((1,), (1,)), ((), ())), preferred_element_type=F32)


def split(v):
    high = v.astype(BF)
    return high, (v - high.astype(F32)).astype(BF)


def kernel(
    tok_ref, refl_ref, gate_hbm, up_hbm, down_hbm, gout_ref, mixed_ref, grad_ref,
    gate_v, up_v, down_v, tok_all, gout_all, tok_t, refl_t, gram_v, inv_v,
    gp_send, gp_xr, gp_zs, gp_zr, gp_all,
    rg_hi, rg_lo, base_v, coef_hi, coef_lo, coef_t,
    p_send, p_xr, p_own, p_zs, p_zr, pre_v,
    h_all,
    mx_cs, mx_cr, mx_own, mx_ys, mx_yr, mx_zs, mx_zr,
    dc_cs, dc_cr, dc_own, dc_ys, dc_yr, dc_zs, dc_zr, dc_xs, dc_xr, dc_hs, dc_hr, dp_all,
    g_cs, g_cr, g_own, g_ys, g_yr, g_zs, g_zr, g_all,
    load_sem, send_sem, recv_sem,
):
    dp = lax.axis_index("dp")
    ten = lax.axis_index("tensor")
    core = lax.rem(dp, 2)
    y = lax.rem(dp // 2, 4)
    zl = dp // 8
    x = lax.rem(ten, 4)
    zh = ten // 4

    def to_x(i):
        return (dp, zh * 4 + lax.rem(x + i, 4))

    def to_zh():
        return (dp, (1 - zh) * 4 + x)

    def to_y(i):
        return ((zl * 4 + lax.rem(y + i, 4)) * 2 + core, ten)

    def to_zl(i):
        return ((lax.rem(zl + i, 4) * 4 + y) * 2 + core, ten)

    def to_core():
        return ((zl * 4 + y) * 2 + 1 - core, ten)

    peers = [to_x(1), to_x(2), to_x(3), to_zh(), to_y(1), to_y(2), to_y(3)]
    peers += [to_zl(1), to_zl(2), to_zl(3), to_core()]

    copies = []

    def send(src, dst, device):
        at = len(copies)
        copy = pltpu.make_async_remote_copy(
            src_ref=src,
            dst_ref=dst,
            send_sem=send_sem.at[at],
            recv_sem=recv_sem.at[at],
            device_id=device,
            device_id_type=MESH,
        )
        copy.start()
        copies.append(copy)
        return copy

    def land(batch):
        for copy in batch:
            copy.wait_recv()

    def rows_own(n):
        return pl.ds(pl.multiple_of((core * 16 + y * 4 + zl) * n, n), n)

    def rows_y(n):
        return pl.ds(pl.multiple_of((core * 16 + y * 4) * n, 4 * n), 4 * n)

    def rows_core(n):
        return pl.ds(pl.multiple_of(core * 16 * n, 16 * n), 16 * n)

    def gather_zl(buf, n):
        return [send(buf.at[rows_own(n)], buf.at[rows_own(n)], to_zl(i)) for i in (1, 2, 3)]

    def gather_y(buf, n):
        return [send(buf.at[rows_y(n)], buf.at[rows_y(n)], to_y(i)) for i in (1, 2, 3)]

    def gather_core(buf, n):
        return [send(buf.at[rows_core(n)], buf.at[rows_core(n)], to_core())]

    loads = [
        pltpu.make_async_copy(src, dst, load_sem.at[i])
        for i, (src, dst) in enumerate(((down_hbm, down_v), (gate_hbm, gate_v), (up_hbm, up_v)))
    ]
    for load in loads:
        load.start()

    barrier = pltpu.get_barrier_semaphore()
    for peer in peers:
        pl.semaphore_signal(barrier, inc=1, device_id=peer, device_id_type=MESH)
    tok_all[rows_own(TB), :] = tok_ref[...]
    gout_all[rows_own(TB), :] = gout_ref[...]
    pl.semaphore_wait(barrier, len(peers))

    gout_zl = gather_zl(gout_all, TB)
    tok_zl = gather_zl(tok_all, TB)

    proj = jnp.dot(tok_ref[...].astype(F32), refl_ref[...], precision=HI, preferred_element_type=F32)
    gp_send[0:TB, :] = proj
    refl_t[...] = jnp.transpose(refl_ref[...])
    gram_v[...] = jnp.dot(refl_t[...], refl_ref[...], precision=HI, preferred_element_type=F32)
    gp_send[TB:, :] = gram_v[rows_own(GB), :]
    gp_x = [send(gp_send, gp_xr.at[i - 1], to_x(i)) for i in (1, 2, 3)]

    land(gout_zl)
    gout_y = gather_y(gout_all, TB)
    land(tok_zl)
    tok_y = gather_y(tok_all, TB)

    land(gp_x)
    gp_zs[...] = gp_send[...] + gp_xr[0] + gp_xr[1] + gp_xr[2]
    gp_z = send(gp_zs, gp_zr, to_zh())

    land(gout_y)
    gout_core = gather_core(gout_all, TB)

    weights = (gate_v, up_v)
    loads[1].wait()
    loads[2].wait()
    t_hi, t_lo = split(refl_t[...])
    for u in range(2):
        rg = nn(t_hi, weights[u][...]) + nn(t_lo, weights[u][...])
        hi, lo = split(rg)
        rg_hi[u] = hi
        rg_lo[u] = lo

    gp_z.wait_recv()
    own_q = core * 16 + y * 4 + zl
    gp_all[own_q] = gp_zs[...] + gp_zr[...]
    gp_zl = gather_zl(gp_all, 1)

    loads[0].wait()
    land(gout_core)

    def x_rows(i):
        return pl.ds(pl.multiple_of(lax.rem(x + i, 4) * 128, 128), 128)

    def reduce_x(u, block):
        started = []
        for i in (2, 1, 3):
            p_send[u, x_rows(i), :] = block(x_rows(i)).astype(BF)
            started.append(send(p_send.at[u, x_rows(i)], p_xr.at[u, i - 1], to_x(i)))
        p_own[u] = block(x_rows(0))
        return started

    def reduce_zh(u, started):
        land(started)
        total = p_own.at[u]
        total[...] = (
            total[...] + p_xr[u, 0].astype(F32) + p_xr[u, 1].astype(F32) + p_xr[u, 2].astype(F32)
        )
        other = pl.ds(pl.multiple_of((1 - zh) * 64, 64), 64)
        p_zs[u] = p_own[u, other, :].astype(BF)
        return send(p_zs.at[u], p_zr.at[u], to_zh())

    def reduced(u, started):
        started.wait_recv()
        mine = pl.ds(pl.multiple_of(zh * 64, 64), 64)
        return p_own[u, mine, :] + p_zr[u].astype(F32)

    dh_x = reduce_x(2, lambda rows: nt(gout_all[rows, :], down_v[...]))

    land(gp_zl)
    gp_y = gather_y(gp_all, 1)
    land(tok_y)
    tok_core = gather_core(tok_all, TB)

    land(tok_core)
    for u in range(2):
        w = weights[u]

        def product(i, carry, u=u, w=w):
            rows = pl.ds(pl.multiple_of(i * 256, 256), 256)
            base_v[u, rows, :] = nn(tok_all[rows, :], w[...])
            return carry

        lax.fori_loop(0, 2, product, 0)

    land(gp_y)
    gp_core = gather_core(gp_all, 1)
    dh_z = reduce_zh(2, dh_x)
    land(gp_core)

    gram = gp_all[:, TB:, :].reshape(R, R)
    row = lax.broadcasted_iota(jnp.int32, (R, R), 0)
    col = lax.broadcasted_iota(jnp.int32, (R, R), 1)
    eye = row == col
    diag_col = 0.5 * jnp.sum(jnp.where(eye, gram, 0.0), axis=1, keepdims=True)
    diag_row = 0.5 * jnp.sum(jnp.where(eye, gram, 0.0), axis=0, keepdims=True)
    gram_v[...] = jnp.where(col > row, gram, 0.0) / diag_col
    first = (col == row + 1) & ((row & 1) == 0)
    inv_v[...] = jnp.where(eye, 1.0, 0.0) - jnp.where(first, gram_v[...], 0.0)

    def double(level, carry):
        rb = lax.shift_right_logical(row, level)
        cb = lax.shift_right_logical(col, level)
        corner = (cb == rb + 1) & ((rb & 1) == 0)
        m = jnp.where(corner, gram_v[...], 0.0)
        half = jnp.dot(m, inv_v[...], precision=HI, preferred_element_type=F32)
        inv_v[...] -= jnp.dot(inv_v[...], half, precision=HI, preferred_element_type=F32)
        return carry

    lax.fori_loop(1, 8, double, 0)
    inv_v[...] = inv_v[...] / diag_row

    proj_all = gp_all[:, :TB, :].reshape(TOKENS, R)
    coeffs = jnp.dot(proj_all, inv_v[...], precision=HI, preferred_element_type=F32)
    hi, lo = split(coeffs)
    coef_hi[...] = hi
    coef_lo[...] = lo

    def pre_block(u):
        def block(rows):
            ch = coef_hi[rows, :]
            moved = nn(ch, rg_hi[u]) + nn(ch, rg_lo[u]) + nn(coef_lo[rows, :], rg_hi[u])
            return base_v[u, rows, :] - moved

        return block

    gate_x = reduce_x(0, pre_block(0))
    up_x = reduce_x(1, pre_block(1))

    coef_t[...] = jnp.transpose(coeffs)
    tok_t[...] = jnp.transpose(tok_all[...])
    d_hidden = reduced(2, dh_z)
    pre_v[2] = d_hidden

    gate_z = reduce_zh(0, gate_x)
    up_z = reduce_zh(1, up_x)
    pre_v[0] = reduced(0, gate_z)
    pre_v[1] = reduced(1, up_z)

    gate = pre_v[0]
    up = pre_v[1]
    d_hidden = pre_v[2]
    sigma = jax.nn.sigmoid(gate)
    share = pl.ds(pl.multiple_of(x * 128 + zh * 64, 64), 64)
    other = pl.ds(pl.multiple_of(x * 128 + (1 - zh) * 64, 64), 64)
    h_all[0, share, :] = (d_hidden * up * sigma * (1.0 + gate * (1.0 - sigma))).astype(BF)
    h_all[1, share, :] = (d_hidden * gate * sigma).astype(BF)
    h_all[2, share, :] = (gate * sigma * up).astype(BF)

    h_z, h_x, h_x2 = [], [], []
    for u in range(3):
        h_z.append(send(h_all.at[u, share], h_all.at[u, share], to_zh()))
        h_x.append([send(h_all.at[u, share], h_all.at[u, share], to_x(i)) for i in (2, 1, 3)])
    for u in range(3):
        h_z[u].wait_recv()
        h_x2.append([send(h_all.at[u, other], h_all.at[u, other], to_x(i)) for i in (2, 1, 3)])

    def land_unit(u):
        land(h_x[u])
        land(h_x2[u])

    half_own = pl.ds(pl.multiple_of(core * 256, 256), 256)
    half_other = pl.ds(pl.multiple_of((1 - core) * 256, 256), 256)

    land_unit(0)
    land_unit(1)

    def dc_block(rows):
        total = nt(h_all[0, rows, :], rg_hi[0]) + nt(h_all[0, rows, :], rg_lo[0])
        return total + nt(h_all[1, rows, :], rg_hi[1]) + nt(h_all[1, rows, :], rg_lo[1])

    def scatter_y(own, sent, got, n, dtype):
        started = []
        for i in (2, 1, 3):
            rows = pl.ds(pl.multiple_of(lax.rem(y + i, 4) * 4 * n, 4 * n), 4 * n)
            sent[i - 1] = own[rows, :].astype(dtype)
            started.append(send(sent.at[i - 1], got.at[i - 1], to_y(i)))
        return started

    def after_y(own, got, started, n):
        land(started)
        rows = pl.ds(pl.multiple_of(y * 4 * n, 4 * n), 4 * n)
        own[rows, :] = own[rows, :] + got[0].astype(F32) + got[1].astype(F32) + got[2].astype(F32)

    def scatter_zl(own, sent, got, n, dtype):
        started = []
        for i in (2, 1, 3):
            rows = pl.ds(pl.multiple_of((y * 4 + lax.rem(zl + i, 4)) * n, n), n)
            sent[i - 1] = own[rows, :].astype(dtype)
            started.append(send(sent.at[i - 1], got.at[i - 1], to_zl(i)))
        return started

    def after_zl(own, got, started, n):
        land(started)
        rows = pl.ds(pl.multiple_of((y * 4 + zl) * n, n), n)
        return own[rows, :] + got[0].astype(F32) + got[1].astype(F32) + got[2].astype(F32)

    dc_cs[...] = dc_block(half_other)
    dc_c = send(dc_cs, dc_cr, to_core())
    dc_own[...] = dc_block(half_own)
    dc_c.wait_recv()
    dc_own[...] = dc_own[...] + dc_cr[...]
    dc_y = scatter_y(dc_own, dc_ys, dc_yr, TB, F32)

    t_hi, t_lo = split(coef_t[...])
    q0_hi, q0_lo = split(nn(t_hi, h_all[0]) + nn(t_lo, h_all[0]))
    q1_hi, q1_lo = split(nn(t_hi, h_all[1]) + nn(t_lo, h_all[1]))

    def g_block(rows):
        total = nt(gate_v[rows, :], q0_hi) + nt(gate_v[rows, :], q0_lo)
        return -(total + nt(up_v[rows, :], q1_hi) + nt(up_v[rows, :], q1_lo))

    g_half_own = pl.ds(pl.multiple_of(core * 512, 512), 512)
    g_half_other = pl.ds(pl.multiple_of((1 - core) * 512, 512), 512)
    g_cs[...] = g_block(g_half_other).astype(BF)
    g_c = send(g_cs, g_cr, to_core())

    after_y(dc_own, dc_yr, dc_y, TB)
    dc_z = scatter_zl(dc_own, dc_zs, dc_zr, TB, F32)

    g_own[...] = g_block(g_half_own)
    g_c.wait_recv()
    g_own[...] = g_own[...] + g_cr[...].astype(F32)
    g_y = scatter_y(g_own, g_ys, g_yr, DO, BF)

    dc_xs[...] = after_zl(dc_own, dc_zr, dc_z, TB)
    dc_x = [send(dc_xs, dc_xr.at[i - 1], to_x(i)) for i in (1, 2, 3)]

    land_unit(2)
    mx_cs[...] = nn(h_all[2, half_other, :], down_v[...]).astype(BF)
    mx_c = send(mx_cs, mx_cr, to_core())

    land(dc_x)
    dc_hs[...] = dc_xs[...] + dc_xr[0] + dc_xr[1] + dc_xr[2]
    dc_h = send(dc_hs, dc_hr, to_zh())

    after_y(g_own, g_yr, g_y, DO)
    g_z = scatter_zl(g_own, g_zs, g_zr, DO, BF)

    mx_own[...] = nn(h_all[2, half_own, :], down_v[...])
    mx_c.wait_recv()
    mx_own[...] = mx_own[...] + mx_cr[...].astype(F32)
    mx_y = scatter_y(mx_own, mx_ys, mx_yr, TB, BF)

    dc_h.wait_recv()
    d_coeffs = -(dc_hs[...] + dc_hr[...])
    dp_all[rows_own(TB), :] = lax.dot_general(
        d_coeffs, inv_v[...], (((1,), (1,)), ((), ())), precision=HI, preferred_element_type=F32
    )
    dp_zl = gather_zl(dp_all, TB)

    g_all[rows_own(DO), :] = after_zl(g_own, g_zr, g_z, DO).astype(BF)
    g_zl = gather_zl(g_all, DO)

    land(dp_zl)
    dp_y = gather_y(dp_all, TB)

    after_y(mx_own, mx_yr, mx_y, TB)
    mx_z = scatter_zl(mx_own, mx_zs, mx_zr, TB, BF)

    land(g_zl)
    g_y2 = gather_y(g_all, DO)

    land(dp_y)
    dp_core = gather_core(dp_all, TB)
    mixed_ref[...] = after_zl(mx_own, mx_zr, mx_z, TB).astype(BF)
    land(dp_core)

    d_coupling = -jnp.dot(coef_t[...], dp_all[...], precision=HI, preferred_element_type=F32)
    sym = jnp.where(col >= row, d_coupling, jnp.transpose(d_coupling))
    d_hi, d_lo = split(dp_all[...])
    land(g_y2)
    g_core = gather_core(g_all, DO)
    total = nn(tok_t[...], d_hi) + nn(tok_t[...], d_lo)
    total = total + jnp.dot(refl_ref[...], sym, precision=HI, preferred_element_type=F32)
    land(g_core)
    grad_ref[...] = total + g_all[...].astype(F32)

    for copy in copies:
        copy.wait_send()


def scratch():
    v = pltpu.VMEM
    dma = pltpu.SemaphoreType.DMA
    own = TB + GB
    return [
        v((DB, FB), BF), v((DB, FB), BF), v((FB, DB), BF),
        v((TOKENS, DB), BF), v((TOKENS, DB), BF), v((DB, TOKENS), BF), v((R, DB), F32), v((R, R), F32), v((R, R), F32),
        v((own, R), F32), v((3, own, R), F32), v((own, R), F32), v((own, R), F32), v((32, own, R), F32),
        v((2, R, FB), BF), v((2, R, FB), BF), v((2, TOKENS, FB), F32),
        v((TOKENS, R), BF), v((TOKENS, R), BF), v((R, TOKENS), F32),
        v((3, TOKENS, FB), BF), v((3, 3, 128, FB), BF), v((3, 128, FB), F32),
        v((3, 64, FB), BF), v((3, 64, FB), BF), v((3, 64, FB), F32),
        v((3, TOKENS, FB), BF),
        v((256, DB), BF), v((256, DB), BF), v((256, DB), F32),
        v((3, 64, DB), BF), v((3, 64, DB), BF), v((3, TB, DB), BF), v((3, TB, DB), BF),
        v((256, R), F32), v((256, R), F32), v((256, R), F32),
        v((3, 64, R), F32), v((3, 64, R), F32), v((3, TB, R), F32), v((3, TB, R), F32),
        v((TB, R), F32), v((3, TB, R), F32), v((TB, R), F32), v((TB, R), F32), v((TOKENS, R), F32),
        v((512, R), BF), v((512, R), BF), v((512, R), F32),
        v((3, 4 * DO, R), BF), v((3, 4 * DO, R), BF), v((3, DO, R), BF), v((3, DO, R), BF), v((DB, R), BF),
        dma((3,)), dma((SEMS,)), dma((SEMS,)),
    ]


def body(tokens, reflectors, gate_weight, up_weight, down_weight, grad_out):
    whole = pl.BlockSpec(memory_space=pltpu.VMEM)
    far = pl.BlockSpec(memory_space=pl.ANY)
    return pl.pallas_call(
        kernel,
        out_shape=(
            jax.ShapeDtypeStruct((TB, DB), BF),
            jax.ShapeDtypeStruct((DB, R), F32),
        ),
        in_specs=[whole, whole, far, far, far, whole],
        out_specs=(whole, whole),
        scratch_shapes=scratch(),
        compiler_params=pltpu.CompilerParams(
            collective_id=0, has_side_effects=True, vmem_limit_bytes=56 << 20
        ),
    )(tokens, reflectors, gate_weight, up_weight, down_weight, grad_out)


def solution(mesh):
    placed = (
        P("dp", "tensor"),
        P("tensor", None),
        P("tensor", "dp"),
        P("tensor", "dp"),
        P("dp", "tensor"),
        P("dp", "tensor"),
    )
    return jax.shard_map(
        body,
        mesh=mesh,
        in_specs=placed,
        out_specs=(P("dp", "tensor"), P("tensor", None)),
        check_vma=False,
    )
```

time: 1010 us -> 154 us (0.15)
  waiting for transfers between devices: 800 us -> 0 us
  Pallas kernels: 0 us -> 149 us
  blocking collectives: 137 us -> 0 us
  matrix products: 41.4 us -> 0 us
  between operations: 15.8 us -> 0.64 us
    psum x2 -> x0, waiting for transfers between devices: 337 us -> none  [the longest x1 282 us: body(): summed_grad, cross = lax.psum((local_grad, local_cross), 'dp')]
    reduce_scatter x4 -> x0, waiting for transfers between devices: 335 us -> none  [the longest x1 122 us: body(): lax.psum_scatter(partial_pre, 'tensor', scatter_dimension=0, tiled=True)]
    pallas_call x0 -> x1, Pallas kernels: none -> 149 us  [body(): pl.pallas_call(kernel, out_shape=(jax.ShapeDtypeStruct((TB, DB), BF), jax...]
    all_gather x3 -> x0, waiting for transfers between devices: 128 us -> none  [the longest x1 69.3 us: body(): d_pre_all = lax.all_gather(d_pre_share, 'tensor', axis=0, tiled=True)]
    psum x2 -> x0, blocking collectives: 96 us -> none  [the longest x1 49.4 us: body(): gram, proj = lax.psum((gram_part, proj_part), 'tensor')]
    dot_general x31 -> x0, matrix products: 41.4 us -> none  [the longest x1 6.23 us: body(): jnp.dot(lax.all_gather(reflected, 'dp', axis=0, tiled=True), weights, pre...]
    all_gather x1 -> x0, blocking collectives: 41.3 us -> none  [body(): hidden_all = lax.all_gather(hidden_share, 'tensor', axis=0, tiled=True)]
  transfers between devices with their start and end apart: 9 -> 0, of which waited for: 8 -> 0; matrix products, arithmetic and copies ran while one was open for 4% -> 0% of each run, Pallas kernels for 0% -> 0%
where the time goes in v1:
time: 154 us
  Pallas kernels  149 us (97%)
  local copies, waits for them, and re-layouts  3.64 us (2%)
    pallas_call x1, Pallas kernels, body(): pl.pallas_call(kernel, out_shape=(jax.ShapeDtypeStruct((TB, DB), BF), jax...  149 us
    unnamed x2, local copies, waits for them, and re-layouts  3.64 us

profile of v1, /device:TPU:1, one launch (start us, length us, event | category | flops | bytes accessed | tf_op | source)
XLA Modules:
  0.0 153.7 jit_solution(6515016983844183259)
XLA Ops:
  0.6 149.4 %shard_map.77 = (bf16[16,1024]{1,0:T(8,128)(2,1)}, f32[1024,256]{1,0:T(8,128)}) custom-call(bf16[16,1024]{1,0:T(8,128)(2,1)} %tok_ref.1, f32[1024,256]{1,0:T(8,128)} %refl_ref.1, bf16[1024,896]{1,0:T(8,128)(2,1)} %gate_hbm.1, bf16[1024,896]{1,0:T(8,128)(2,1)} %up_hbm.1, bf16[896,1024]{1,0:T(8,128)(2,1)} %down_hbm.1, bf16[16,1024]{1,0:T(8,128)(2,1)} %gout_ref.1), custom_call_target="tpu_custom_call" | custom-call | tf_op jit(solution)/shard_map/pallas_call | solution.py:435
  150.1 1.4 copy.10
  151.4 2.3 %copy.11 = f32[1024,256]{1,0:T(8,128)} copy(f32[1024,256]{1,0:T(8,128)} %get-tuple-element.5) | data formatting | bytes 2097152

commit v2 on v1

v2 whole, which is shorter than its diff:
```python
import functools

import jax
import jax.numpy as jnp
from jax import lax
from jax.experimental import pallas as pl
from jax.experimental.pallas import tpu as pltpu
from jax.sharding import PartitionSpec as P

MESH = pl.DeviceIdType.MESH
BF = jnp.bfloat16
F32 = jnp.float32
HI = lax.Precision.HIGHEST

D, FF, R, TOKENS = 8192, 28672, 256, 512
DB = D // 8
FB = FF // 32
TB = TOKENS // 32
DO = DB // 32
SEMS = 224
ALL_COLS = pl.ds(0, FB)
HALVES = (pl.ds(0, 512), pl.ds(512, 384))
COLS = (pl.ds(0, 128), pl.ds(128, 256), pl.ds(384, 256), pl.ds(640, 256))


def nn(a, b):
    return jnp.dot(a, b, preferred_element_type=F32)


def nt(a, b):
    return lax.dot_general(a, b, (((1,), (1,)), ((), ())), preferred_element_type=F32)


def split(v):
    high = v.astype(BF)
    return high, (v - high.astype(F32)).astype(BF)


def kernel(
    tok_hbm, refl_hbm, gate_hbm, up_hbm, down_hbm, gout_hbm, mixed_ref, grad_ref,
    refl_v, gate_v, up_v, down_v, tok_all, gout_all, tok_t, refl_t, gram_v, unit_v, inv_v,
    gram_all, gm_xr, gm_zs, gm_zr, pj_send, pj_xr, pj_zs, pj_zr, pj_all,
    rg_hi, rg_lo, reflected, coef_v, coef_t,
    p_send, p_xr, p_own, p_zs, p_zr,
    h_all,
    mx_cs, mx_cr, mx_own, mx_ys, mx_yr, mx_zs, mx_zr,
    dc_cs, dc_cr, dc_own, dc_ys, dc_yr, dc_zs, dc_zr, dc_xs, dc_xr, dc_hs, dc_hr, dp_all,
    g_cs, g_cr, g_own, g_ys, g_yr, g_zs, g_zr, g_all,
    load_sem, send_sem, recv_sem,
):
    dp = lax.axis_index("dp")
    ten = lax.axis_index("tensor")
    core = lax.rem(dp, 2)
    y = lax.rem(dp // 2, 4)
    zl = dp // 8
    x = lax.rem(ten, 4)
    zh = ten // 4

    def to_x(i):
        return (dp, zh * 4 + lax.rem(x + i, 4))

    def to_zh():
        return (dp, (1 - zh) * 4 + x)

    def to_y(i):
        return ((zl * 4 + lax.rem(y + i, 4)) * 2 + core, ten)

    def to_zl(i):
        return ((lax.rem(zl + i, 4) * 4 + y) * 2 + core, ten)

    def to_core():
        return ((zl * 4 + y) * 2 + 1 - core, ten)

    peers = [to_x(1), to_x(2), to_x(3), to_zh(), to_y(1), to_y(2), to_y(3)]
    peers += [to_zl(1), to_zl(2), to_zl(3), to_core()]

    copies = []

    def send(src, dst, device):
        at = len(copies)
        copy = pltpu.make_async_remote_copy(
            src_ref=src,
            dst_ref=dst,
            send_sem=send_sem.at[at],
            recv_sem=recv_sem.at[at],
            device_id=device,
            device_id_type=MESH,
        )
        copy.start()
        copies.append(copy)
        return copy

    def land(batch):
        for copy in batch:
            copy.wait_recv()

    def rows_own(n):
        return pl.ds(pl.multiple_of((core * 16 + y * 4 + zl) * n, n), n)

    def rows_y(n):
        return pl.ds(pl.multiple_of((core * 16 + y * 4) * n, 4 * n), 4 * n)

    def rows_core(n):
        return pl.ds(pl.multiple_of(core * 16 * n, 16 * n), 16 * n)

    def gather_zl(buf, n):
        return [send(buf.at[rows_own(n)], buf.at[rows_own(n)], to_zl(i)) for i in (1, 2, 3)]

    def gather_y(buf, n):
        return [send(buf.at[rows_y(n)], buf.at[rows_y(n)], to_y(i)) for i in (1, 2, 3)]

    def gather_core(buf, n):
        return [send(buf.at[rows_core(n)], buf.at[rows_core(n)], to_core())]

    def gather_start(buf, n):
        own = buf.at[rows_own(n)]
        along_zl = [send(own, own, to_zl(i)) for i in (1, 2, 3)]
        return along_zl, [send(own, own, to_y(i)) for i in (1, 2, 3)]

    def gather_rest(buf, n, started):
        along_zl, along_y = started
        for i, copy in zip((1, 2, 3), along_zl):
            copy.wait_recv()
            at = core * 16 + y * 4 + lax.rem(zl + 4 - i, 4)
            came = buf.at[pl.ds(pl.multiple_of(at * n, n), n)]
            along_y.extend(send(came, came, to_y(k)) for k in (1, 2, 3))
        return along_y

    loads = [
        pltpu.make_async_copy(src, dst, load_sem.at[i])
        for i, (src, dst) in enumerate(
            (
                (refl_hbm, refl_v),
                (tok_hbm, tok_all.at[rows_own(TB)]),
                (gout_hbm, gout_all.at[rows_own(TB)]),
                (gate_hbm, gate_v),
                (up_hbm, up_v),
                (down_hbm, down_v),
            )
        )
    ]
    for load in loads:
        load.start()

    barrier = pltpu.get_barrier_semaphore()
    for peer in peers:
        pl.semaphore_signal(barrier, inc=1, device_id=peer, device_id_type=MESH)

    loads[2].wait()
    pl.semaphore_wait(barrier, len(peers))
    gout_start = gather_start(gout_all, TB)

    loads[0].wait()
    my_half = pl.ds(pl.multiple_of(core * 128, 128), 128)
    columns = jnp.transpose(refl_v[:, my_half])
    gram_v[my_half, :] = jnp.dot(columns, refl_v[...], precision=HI, preferred_element_type=F32)

    def gram_rows(i):
        return pl.ds(pl.multiple_of(core * 128 + lax.rem(x + i, 4) * 32, 32), 32)

    gram_x = [send(gram_v.at[gram_rows(i)], gm_xr.at[i - 1], to_x(i)) for i in (2, 1, 3)]
    gout_y = gather_rest(gout_all, TB, gout_start)
    loads[1].wait()
    own_tok = tok_all[rows_own(TB), :].astype(F32)
    pj_send[...] = jnp.dot(own_tok, refl_v[...], precision=HI, preferred_element_type=F32)
    pj_x = [send(pj_send, pj_xr.at[i - 1], to_x(i)) for i in (2, 1, 3)]
    tok_zl = gather_zl(tok_all, TB)

    land(gram_x)
    gm_zs[...] = gram_v[gram_rows(0), :] + gm_xr[0] + gm_xr[1] + gm_xr[2]
    gram_z = send(gm_zs, gm_zr, to_zh())
    land(pj_x)
    pj_zs[...] = pj_send[...] + pj_xr[0] + pj_xr[1] + pj_xr[2]
    pj_z = send(pj_zs, pj_zr, to_zh())

    land(gout_y)
    gout_core = gather_core(gout_all, TB)
    land(tok_zl)
    tok_y = gather_y(tok_all, TB)

    def x_rows(i):
        return pl.ds(pl.multiple_of(lax.rem(x + i, 4) * 128, 128), 128)

    def scatter_x(u, cols, block):
        started = []
        for i in (2, 1, 3):
            p_send[u, x_rows(i), cols] = block(x_rows(i), cols).astype(BF)
            started.append(send(p_send.at[u, x_rows(i), cols], p_xr.at[u, i - 1, :, cols], to_x(i)))
        p_own[u, :, cols] = block(x_rows(0), cols)
        return started

    def exchange_zh(u, cols, started):
        land(started)
        got = p_xr[u, 0, :, cols].astype(F32) + p_xr[u, 1, :, cols].astype(F32)
        total = p_own[u, :, cols] + got + p_xr[u, 2, :, cols].astype(F32)
        p_own[u, :, cols] = total
        p_zs[u, :, cols] = total.astype(BF)
        return send(p_zs.at[u, :, cols], p_zr.at[u, :, cols], to_zh())

    def reduced(u, cols, started):
        started.wait_recv()
        return p_own[u, :, cols] + p_zr[u, :, cols].astype(F32)

    def dh_block(rows, cols):
        return nt(gout_all[rows, :], down_v[cols, :])

    loads[5].wait()
    land(gout_core)
    dh_x = [scatter_x(2, HALVES[0], dh_block)]
    gram_z.wait_recv()
    gram_all[gram_rows(0), :] = gm_zs[...] + gm_zr[...]
    own_gram = gram_all.at[gram_rows(0)]
    gram_x = [send(own_gram, own_gram, to_x(i)) for i in (2, 1, 3)]
    pj_z.wait_recv()
    pj_all[rows_own(TB), :] = pj_zs[...] + pj_zr[...]
    pj_start = gather_start(pj_all, TB)
    dh_x.append(scatter_x(2, HALVES[1], dh_block))
    land(gram_x)
    gram_core = send(gram_all.at[my_half], gram_all.at[my_half], to_core())
    pj_y = gather_rest(pj_all, TB, pj_start)
    land(tok_y)
    tok_core = gather_core(tok_all, TB)
    gram_core.wait_recv()

    gram = gram_all[...]
    row = lax.broadcasted_iota(jnp.int32, (R, R), 0)
    col = lax.broadcasted_iota(jnp.int32, (R, R), 1)
    eye = row == col
    diag_col = 0.5 * jnp.sum(jnp.where(eye, gram, 0.0), axis=1, keepdims=True)
    diag_row = 0.5 * jnp.sum(jnp.where(eye, gram, 0.0), axis=0, keepdims=True)
    unit_v[...] = jnp.where(col > row, gram, 0.0) / diag_col
    first = (col == row + 1) & ((row & 1) == 0)
    inv_v[...] = jnp.where(eye, 1.0, 0.0) - jnp.where(first, unit_v[...], 0.0)

    def double(level, carry):
        rb = lax.shift_right_logical(row, level)
        cb = lax.shift_right_logical(col, level)
        corner = (cb == rb + 1) & ((rb & 1) == 0)
        m = jnp.where(corner, unit_v[...], 0.0)
        step = jnp.dot(m, inv_v[...], precision=HI, preferred_element_type=F32)
        inv_v[...] -= jnp.dot(inv_v[...], step, precision=HI, preferred_element_type=F32)
        return carry

    lax.fori_loop(1, 4, double, 0)
    land(pj_y)
    pj_core = gather_core(pj_all, TB)
    dh_z = [exchange_zh(2, HALVES[0], dh_x[0])]
    lax.fori_loop(4, 8, double, 0)
    inv_v[...] = inv_v[...] / diag_row
    land(pj_core)
    coef_v[...] = jnp.dot(pj_all[...], inv_v[...], precision=HI, preferred_element_type=F32)
    land(tok_core)
    r_hi, r_lo = split(refl_v[...])
    weights = (gate_v, up_v)
    loads[3].wait()
    loads[4].wait()

    def reflect(rows):
        c_hi, c_lo = split(coef_v[rows, :])
        moved = nt(c_hi, r_hi) + nt(c_lo, r_hi) + nt(c_hi, r_lo)
        reflected[rows, :] = (tok_all[rows, :].astype(F32) - moved).astype(BF)

    def pre_block(u):
        return lambda rows, cols: nn(reflected[rows, :], weights[u][:, cols])

    parts = range(len(COLS))
    pre_x, pre_z, h_x = {}, {}, {}

    def pre_scatter(j):
        for u in range(2):
            pre_x[u, j] = scatter_x(u, COLS[j], pre_block(u))

    def pre_exchange(j):
        for u in range(2):
            pre_z[u, j] = exchange_zh(u, COLS[j], pre_x[u, j])

    def give(u, cols):
        block = h_all.at[u, x_rows(0), cols]
        return [send(block, block, to_x(i)) for i in (2, 1, 3)]

    def activate(j):
        cols = COLS[j]
        gate = reduced(0, cols, pre_z[0, j])
        up = reduced(1, cols, pre_z[1, j])
        d_hidden = p_own[2, :, cols] + p_zr[2, :, cols].astype(F32)
        sigma = jax.nn.sigmoid(gate)
        h_all[0, x_rows(0), cols] = (d_hidden * up * sigma * (1.0 + gate * (1.0 - sigma))).astype(BF)
        h_all[1, x_rows(0), cols] = (d_hidden * gate * sigma).astype(BF)
        for u in range(2):
            h_x[u, j] = give(u, cols)
        h_all[2, x_rows(0), cols] = (gate * sigma * up).astype(BF)

    pre_x[0, 0], pre_x[1, 0] = [], []
    for i in (2, 1, 3, 0):
        reflect(x_rows(i))
        for u in range(2):
            value = pre_block(u)(x_rows(i), COLS[0])
            if i:
                p_send[u, x_rows(i), COLS[0]] = value.astype(BF)
                pre_x[u, 0].append(
                    send(p_send.at[u, x_rows(i), COLS[0]], p_xr.at[u, i - 1, :, COLS[0]], to_x(i))
                )
            else:
                p_own[u, :, COLS[0]] = value
    dh_z.append(exchange_zh(2, HALVES[1], dh_x[1]))
    pre_scatter(1)
    pre_exchange(0)
    pre_scatter(2)
    pre_exchange(1)
    pre_scatter(3)

    refl_t[...] = jnp.transpose(refl_v[...])
    t_hi, t_lo = split(refl_t[...])
    for u in range(2):
        rg_hi[u], rg_lo[u] = split(nn(t_hi, weights[u][...]) + nn(t_lo, weights[u][...]))
    coef_t[...] = jnp.transpose(coef_v[...])
    tok_t[...] = jnp.transpose(tok_all[...])
    land(dh_z)
    activate(0)
    pre_exchange(2)
    activate(1)
    pre_exchange(3)
    activate(2)
    activate(3)
    for j in parts:
        land(h_x[0, j] + h_x[1, j])

    hidden_x = give(2, ALL_COLS)

    half_own = pl.ds(pl.multiple_of(core * 256, 256), 256)
    half_other = pl.ds(pl.multiple_of((1 - core) * 256, 256), 256)

    def dc_block(rows):
        total = nt(h_all[0, rows, :], rg_hi[0]) + nt(h_all[0, rows, :], rg_lo[0])
        return total + nt(h_all[1, rows, :], rg_hi[1]) + nt(h_all[1, rows, :], rg_lo[1])

    def scatter_y(own, sent, got, n, dtype):
        started = []
        for i in (2, 1, 3):
            rows = pl.ds(pl.multiple_of(lax.rem(y + i, 4) * 4 * n, 4 * n), 4 * n)
            sent[i - 1] = own[rows, :].astype(dtype)
            started.append(send(sent.at[i - 1], got.at[i - 1], to_y(i)))
        return started

    def after_y(own, got, started, n):
        land(started)
        rows = pl.ds(pl.multiple_of(y * 4 * n, 4 * n), 4 * n)
        own[rows, :] = own[rows, :] + got[0].astype(F32) + got[1].astype(F32) + got[2].astype(F32)

    def scatter_zl(own, sent, got, n, dtype):
        started = []
        for i in (2, 1, 3):
            rows = pl.ds(pl.multiple_of((y * 4 + lax.rem(zl + i, 4)) * n, n), n)
            sent[i - 1] = own[rows, :].astype(dtype)
            started.append(send(sent.at[i - 1], got.at[i - 1], to_zl(i)))
        return started

    def after_zl(own, got, started, n):
        land(started)
        rows = pl.ds(pl.multiple_of((y * 4 + zl) * n, n), n)
        return own[rows, :] + got[0].astype(F32) + got[1].astype(F32) + got[2].astype(F32)

    dc_cs[...] = dc_block(half_other)
    dc_c = send(dc_cs, dc_cr, to_core())
    dc_own[...] = dc_block(half_own)
    dc_c.wait_recv()
    dc_own[...] = dc_own[...] + dc_cr[...]
    dc_y = scatter_y(dc_own, dc_ys, dc_yr, TB, F32)

    t_hi, t_lo = split(coef_t[...])
    q0_hi, q0_lo = split(nn(t_hi, h_all[0]) + nn(t_lo, h_all[0]))
    q1_hi, q1_lo = split(nn(t_hi, h_all[1]) + nn(t_lo, h_all[1]))

    def g_block(rows):
        total = nt(gate_v[rows, :], q0_hi) + nt(gate_v[rows, :], q0_lo)
        return -(total + nt(up_v[rows, :], q1_hi) + nt(up_v[rows, :], q1_lo))

    g_half_own = pl.ds(pl.multiple_of(core * 512, 512), 512)
    g_half_other = pl.ds(pl.multiple_of((1 - core) * 512, 512), 512)
    g_cs[...] = g_block(g_half_other).astype(BF)
    g_c = send(g_cs, g_cr, to_core())

    after_y(dc_own, dc_yr, dc_y, TB)
    dc_z = scatter_zl(dc_own, dc_zs, dc_zr, TB, F32)

    g_own[...] = g_block(g_half_own)
    g_c.wait_recv()
    g_own[...] = g_own[...] + g_cr[...].astype(F32)
    g_y = scatter_y(g_own, g_ys, g_yr, DO, BF)

    dc_xs[...] = after_zl(dc_own, dc_zr, dc_z, TB)
    dc_x = [send(dc_xs, dc_xr.at[i - 1], to_x(i)) for i in (1, 2, 3)]

    land(dc_x)
    dc_hs[...] = dc_xs[...] + dc_xr[0] + dc_xr[1] + dc_xr[2]
    dc_h = send(dc_hs, dc_hr, to_zh())

    land(hidden_x)
    mx_cs[...] = nn(h_all[2, half_other, :], down_v[...]).astype(BF)
    mx_c = send(mx_cs, mx_cr, to_core())

    after_y(g_own, g_yr, g_y, DO)
    g_z = scatter_zl(g_own, g_zs, g_zr, DO, BF)

    mx_own[...] = nn(h_all[2, half_own, :], down_v[...])
    mx_c.wait_recv()
    mx_own[...] = mx_own[...] + mx_cr[...].astype(F32)
    mx_y = scatter_y(mx_own, mx_ys, mx_yr, TB, BF)

    dc_h.wait_recv()
    d_coeffs = -(dc_hs[...] + dc_hr[...])
    dp_all[rows_own(TB), :] = lax.dot_general(
        d_coeffs, inv_v[...], (((1,), (1,)), ((), ())), precision=HI, preferred_element_type=F32
    )
    dp_zl = gather_zl(dp_all, TB)

    g_all[rows_own(DO), :] = after_zl(g_own, g_zr, g_z, DO).astype(BF)
    g_zl = gather_zl(g_all, DO)

    land(dp_zl)
    dp_y = gather_y(dp_all, TB)

    after_y(mx_own, mx_yr, mx_y, TB)
    mx_z = scatter_zl(mx_own, mx_zs, mx_zr, TB, BF)

    land(g_zl)
    g_y2 = gather_y(g_all, DO)

    land(dp_y)
    dp_core = gather_core(dp_all, TB)
    mixed_ref[...] = after_zl(mx_own, mx_zr, mx_z, TB).astype(BF)
    land(dp_core)

    d_coupling = -jnp.dot(coef_t[...], dp_all[...], precision=HI, preferred_element_type=F32)
    sym = jnp.where(col >= row, d_coupling, jnp.transpose(d_coupling))
    d_hi, d_lo = split(dp_all[...])
    land(g_y2)
    g_core = gather_core(g_all, DO)
    total = nn(tok_t[...], d_hi) + nn(tok_t[...], d_lo)
    total = total + jnp.dot(refl_v[...], sym, precision=HI, preferred_element_type=F32)
    land(g_core)
    grad_ref[...] = total + g_all[...].astype(F32)

    for copy in copies:
        copy.wait_send()


def scratch():
    v = pltpu.VMEM
    dma = pltpu.SemaphoreType.DMA
    return [
        v((DB, R), F32), v((DB, FB), BF), v((DB, FB), BF), v((FB, DB), BF),
        v((TOKENS, DB), BF), v((TOKENS, DB), BF), v((DB, TOKENS), BF), v((R, DB), F32), v((R, R), F32), v((R, R), F32), v((R, R), F32),
        v((R, R), F32), v((3, 32, R), F32), v((32, R), F32), v((32, R), F32),
        v((TB, R), F32), v((3, TB, R), F32), v((TB, R), F32), v((TB, R), F32), v((TOKENS, R), F32),
        v((2, R, FB), BF), v((2, R, FB), BF), v((TOKENS, DB), BF), v((TOKENS, R), F32), v((R, TOKENS), F32),
        v((3, TOKENS, FB), BF), v((3, 3, 128, FB), BF), v((3, 128, FB), F32), v((3, 128, FB), BF), v((3, 128, FB), BF),
        v((3, TOKENS, FB), BF),
        v((256, DB), BF), v((256, DB), BF), v((256, DB), F32),
        v((3, 64, DB), BF), v((3, 64, DB), BF), v((3, TB, DB), BF), v((3, TB, DB), BF),
        v((256, R), F32), v((256, R), F32), v((256, R), F32),
        v((3, 64, R), F32), v((3, 64, R), F32), v((3, TB, R), F32), v((3, TB, R), F32),
        v((TB, R), F32), v((3, TB, R), F32), v((TB, R), F32), v((TB, R), F32), v((TOKENS, R), F32),
        v((512, R), BF), v((512, R), BF), v((512, R), F32),
        v((3, 4 * DO, R), BF), v((3, 4 * DO, R), BF), v((3, DO, R), BF), v((3, DO, R), BF), v((DB, R), BF),
        dma((6,)), dma((SEMS,)), dma((SEMS,)),
    ]


def body(tokens, reflectors, gate_weight, up_weight, down_weight, grad_out):
    whole = pl.BlockSpec(memory_space=pltpu.VMEM)
    far = pl.BlockSpec(memory_space=pltpu.HBM)
    return pl.pallas_call(
        kernel,
        out_shape=(
            jax.ShapeDtypeStruct((TB, DB), BF),
            jax.ShapeDtypeStruct((DB, R), F32),
        ),
        in_specs=[far] * 6,
        out_specs=(whole, whole),
        scratch_shapes=scratch(),
        compiler_params=pltpu.CompilerParams(
            collective_id=0, has_side_effects=True, vmem_limit_bytes=52 << 20
        ),
    )(tokens, reflectors, gate_weight, up_weight, down_weight, grad_out)


def solution(mesh):
    placed = (
        P("dp", "tensor"),
        P("tensor", None),
        P("tensor", "dp"),
        P("tensor", "dp"),
        P("dp", "tensor"),
        P("dp", "tensor"),
    )
    return jax.shard_map(
        body,
        mesh=mesh,
        in_specs=placed,
        out_specs=(P("dp", "tensor"), P("tensor", None)),
        check_vma=False,
    )
```

time: 154 us -> 128 us (0.83)
  Pallas kernels: 149 us -> 124 us
    pallas_call x1, Pallas kernels: 149 us -> 124 us  [body(): pl.pallas_call(kernel, out_shape=(jax.ShapeDtypeStruct((TB, DB), BF), jax...]
    unnamed x2 -> x6, local copies, waits for them, and re-layouts: 3.64 us -> 3.1 us
where the time goes in v2:
time: 128 us
  Pallas kernels  124 us (97%)
  local copies, waits for them, and re-layouts  3.1 us (2%)
    pallas_call x1, Pallas kernels, body(): pl.pallas_call(kernel, out_shape=(jax.ShapeDtypeStruct((TB, DB), BF), jax...  124 us
    unnamed x6, local copies, waits for them, and re-layouts  3.1 us

profile of v2, /device:TPU:1, one launch (start us, length us, event | category | flops | bytes accessed | tf_op | source)
XLA Modules:
  0.0 128.1 jit_solution(8268674305683529792)
XLA Ops:
  0.6 0.0 copy-start
  0.6 0.7 copy-done
  1.4 0.0 copy-start.1
  1.4 0.8 copy-done.1
  2.1 124.3 %shard_map.77 = (bf16[16,1024]{1,0:T(8,128)(2,1)S(1)}, f32[1024,256]{1,0:T(8,128)S(1)}) custom-call(bf16[16,1024]{1,0:T(8,128)(2,1)S(1)} %copy-done, f32[1024,256]{1,0:T(8,128)} %refl_hbm.1, bf16[1024,896]{1,0:T(8,128)(2,1)} %gate_hbm.1, bf16[1024,896]{1,0:T(8,128)(2,1)} %up_hbm.1, bf16[896,1024]{1,0:T(8,128)(2,1)} %down_hbm.1, bf16[16,1024]{1,0:T(8,128)(2,1)S(1)} %copy-done.1), custom_call_target="tpu_custom_call" | custom-call | tf_op jit(solution)/shard_map/pallas_call | solution.py:473
  126.5 0.6 copy.10
  127.1 1.0 copy.11
Async XLA Ops:
  0.6 0.8 copy-start
  1.4 0.8 copy-start.1

commit v3 on v2

--- a/solution.py
+++ b/solution.py
@@ -42,7 +42,7 @@
     gram_all, gm_xr, gm_zs, gm_zr, pj_send, pj_xr, pj_zs, pj_zr, pj_all,
     rg_hi, rg_lo, reflected, coef_v, coef_t,
     p_send, p_xr, p_own, p_zs, p_zr,
-    h_all,
+    h_all, dc_acc, q_hi, q_lo,
     mx_cs, mx_cr, mx_own, mx_ys, mx_yr, mx_zs, mx_zr,
     dc_cs, dc_cr, dc_own, dc_ys, dc_yr, dc_zs, dc_zr, dc_xs, dc_xr, dc_hs, dc_hr, dp_all,
     g_cs, g_cr, g_own, g_ys, g_yr, g_zs, g_zr, g_all,
@@ -177,6 +177,13 @@
     gout_core = gather_core(gout_all, TB)
     land(tok_zl)
     tok_y = gather_y(tok_all, TB)
+    gram_z.wait_recv()
+    gram_all[gram_rows(0), :] = gm_zs[...] + gm_zr[...]
+    own_gram = gram_all.at[gram_rows(0)]
+    gram_x = [send(own_gram, own_gram, to_x(i)) for i in (2, 1, 3)]
+    pj_z.wait_recv()
+    pj_all[rows_own(TB), :] = pj_zs[...] + pj_zr[...]
+    pj_start = gather_start(pj_all, TB)
 
     def x_rows(i):
         return pl.ds(pl.multiple_of(lax.rem(x + i, 4) * 128, 128), 128)
@@ -207,16 +214,9 @@
     loads[5].wait()
     land(gout_core)
     dh_x = [scatter_x(2, HALVES[0], dh_block)]
-    gram_z.wait_recv()
-    gram_all[gram_rows(0), :] = gm_zs[...] + gm_zr[...]
-    own_gram = gram_all.at[gram_rows(0)]
-    gram_x = [send(own_gram, own_gram, to_x(i)) for i in (2, 1, 3)]
-    pj_z.wait_recv()
-    pj_all[rows_own(TB), :] = pj_zs[...] + pj_zr[...]
-    pj_start = gather_start(pj_all, TB)
-    dh_x.append(scatter_x(2, HALVES[1], dh_block))
     land(gram_x)
     gram_core = send(gram_all.at[my_half], gram_all.at[my_half], to_core())
+    dh_x.append(scatter_x(2, HALVES[1], dh_block))
     pj_y = gather_rest(pj_all, TB, pj_start)
     land(tok_y)
     tok_core = gather_core(tok_all, TB)
@@ -263,7 +263,7 @@
     def pre_block(u):
         return lambda rows, cols: nn(reflected[rows, :], weights[u][:, cols])
 
-    parts = range(len(COLS))
+    last = len(COLS) - 1
     pre_x, pre_z, h_x = {}, {}, {}
 
     def pre_scatter(j):
@@ -277,6 +277,22 @@
     def give(u, cols):
         block = h_all.at[u, x_rows(0), cols]
         return [send(block, block, to_x(i)) for i in (2, 1, 3)]
+
+    def half(i, h):
+        return pl.ds(pl.multiple_of(lax.rem(x + i, 4) * 128 + h * 64, 64), 64)
+
+    def give_sides(u, cols):
+        block = h_all.at[u, x_rows(0), cols]
+        return [send(block, block, to_x(i)) for i in (1, 3)]
+
+    def onward(j):
+        for u in range(2):
+            for i, copy in zip((1, 3), h_x[u, j]):
+                copy.wait_recv()
+                block = h_all.at[u, half(4 - i, i // 2), COLS[j]]
+                h_on.append(send(block, block, to_x(i)))
+
+    h_on = []
 
     def activate(j):
         cols = COLS[j]
@@ -287,7 +303,7 @@
         h_all[0, x_rows(0), cols] = (d_hidden * up * sigma * (1.0 + gate * (1.0 - sigma))).astype(BF)
         h_all[1, x_rows(0), cols] = (d_hidden * gate * sigma).astype(BF)
         for u in range(2):
-            h_x[u, j] = give(u, cols)
+            h_x[u, j] = give(u, cols) if j == last else give_sides(u, cols)
         h_all[2, x_rows(0), cols] = (gate * sigma * up).astype(BF)
 
     pre_x[0, 0], pre_x[1, 0] = [], []
@@ -320,10 +336,34 @@
     pre_exchange(2)
     activate(1)
     pre_exchange(3)
+    onward(0)
     activate(2)
+    onward(1)
     activate(3)
-    for j in parts:
-        land(h_x[0, j] + h_x[1, j])
+    onward(2)
+
+    t_hi, t_lo = split(coef_t[...])
+
+    def dc_part(rows, j):
+        cols = COLS[j]
+        total = jnp.zeros((rows.size, R), F32)
+        for u in range(2):
+            block = h_all[u, rows, cols]
+            total = total + nt(block, rg_hi[u, :, cols]) + nt(block, rg_lo[u, :, cols])
+        return total
+
+    def q_part(j):
+        cols = COLS[j]
+        for u in range(2):
+            block = h_all[u, :, cols]
+            q_hi[u, :, cols], q_lo[u, :, cols] = split(nn(t_hi, block) + nn(t_lo, block))
+
+    everything = pl.ds(0, TOKENS)
+    for j in range(last):
+        land(h_on[4 * j : 4 * j + 4])
+        dc_acc[...] = dc_part(everything, j) if j == 0 else dc_acc[...] + dc_part(everything, j)
+        q_part(j)
+    land(h_x[0, last] + h_x[1, last])
 
     hidden_x = give(2, ALL_COLS)
 
@@ -331,8 +371,7 @@
     half_other = pl.ds(pl.multiple_of((1 - core) * 256, 256), 256)
 
     def dc_block(rows):
-        total = nt(h_all[0, rows, :], rg_hi[0]) + nt(h_all[0, rows, :], rg_lo[0])
-        return total + nt(h_all[1, rows, :], rg_hi[1]) + nt(h_all[1, rows, :], rg_lo[1])
+        return dc_acc[rows, :] + dc_part(rows, last)
 
     def scatter_y(own, sent, got, n, dtype):
         started = []
@@ -367,13 +406,11 @@
     dc_own[...] = dc_own[...] + dc_cr[...]
     dc_y = scatter_y(dc_own, dc_ys, dc_yr, TB, F32)
 
-    t_hi, t_lo = split(coef_t[...])
-    q0_hi, q0_lo = split(nn(t_hi, h_all[0]) + nn(t_lo, h_all[0]))
-    q1_hi, q1_lo = split(nn(t_hi, h_all[1]) + nn(t_lo, h_all[1]))
+    q_part(last)
 
     def g_block(rows):
-        total = nt(gate_v[rows, :], q0_hi) + nt(gate_v[rows, :], q0_lo)
-        return -(total + nt(up_v[rows, :], q1_hi) + nt(up_v[rows, :], q1_lo))
+        total = nt(gate_v[rows, :], q_hi[0]) + nt(gate_v[rows, :], q_lo[0])
+        return -(total + nt(up_v[rows, :], q_hi[1]) + nt(up_v[rows, :], q_lo[1]))
 
     g_half_own = pl.ds(pl.multiple_of(core * 512, 512), 512)
     g_half_other = pl.ds(pl.multiple_of((1 - core) * 512, 512), 512)
@@ -455,7 +492,7 @@
         v((TB, R), F32), v((3, TB, R), F32), v((TB, R), F32), v((TB, R), F32), v((TOKENS, R), F32),
         v((2, R, FB), BF), v((2, R, FB), BF), v((TOKENS, DB), BF), v((TOKENS, R), F32), v((R, TOKENS), F32),
         v((3, TOKENS, FB), BF), v((3, 3, 128, FB), BF), v((3, 128, FB), F32), v((3, 128, FB), BF), v((3, 128, FB), BF),
-        v((3, TOKENS, FB), BF),
+        v((3, TOKENS, FB), BF), v((TOKENS, R), F32), v((2, R, FB), BF), v((2, R, FB), BF),
         v((256, DB), BF), v((256, DB), BF), v((256, DB), F32),
         v((3, 64, DB), BF), v((3, 64, DB), BF), v((3, TB, DB), BF), v((3, TB, DB), BF),
         v((256, R), F32), v((256, R), F32), v((256, R), F32),

time: 128 us -> 123 us (0.961)
  Pallas kernels: 124 us -> 119 us
    pallas_call x1, Pallas kernels: 124 us -> 119 us  [body(): pl.pallas_call(kernel, out_shape=(jax.ShapeDtypeStruct((TB, DB), BF), jax...]
where the time goes in v3:
time: 123 us; the launch traced here: 122 us
  Pallas kernels  119 us (97%)
  local copies, waits for them, and re-layouts  3.1 us (3%)
    pallas_call x1, Pallas kernels, body(): pl.pallas_call(kernel, out_shape=(jax.ShapeDtypeStruct((TB, DB), BF), jax...  119 us
    unnamed x6, local copies, waits for them, and re-layouts  3.1 us

profile of v3, /device:TPU:1, one launch (start us, length us, event | category | flops | bytes accessed | tf_op | source)
XLA Modules:
  0.0 122.3 jit_solution(14205923028683063914)
XLA Ops:
  0.6 0.0 copy-start
  0.6 0.7 copy-done
  1.4 0.0 copy-start.1
  1.4 0.8 copy-done.1
  2.1 118.6 %shard_map.77 = (bf16[16,1024]{1,0:T(8,128)(2,1)S(1)}, f32[1024,256]{1,0:T(8,128)S(1)}) custom-call(bf16[16,1024]{1,0:T(8,128)(2,1)S(1)} %copy-done, f32[1024,256]{1,0:T(8,128)} %refl_hbm.1, bf16[1024,896]{1,0:T(8,128)(2,1)} %gate_hbm.1, bf16[1024,896]{1,0:T(8,128)(2,1)} %up_hbm.1, bf16[896,1024]{1,0:T(8,128)(2,1)} %down_hbm.1, bf16[16,1024]{1,0:T(8,128)(2,1)S(1)} %copy-done.1), custom_call_target="tpu_custom_call" | custom-call | tf_op jit(solution)/shard_map/pallas_call | solution.py:510
  120.7 0.6 copy.10
  121.3 1.0 copy.11
Async XLA Ops:
  0.6 0.8 copy-start
  1.4 0.8 copy-start.1

commit v4 on v3

--- a/solution.py
+++ b/solution.py
@@ -247,6 +247,7 @@
     dh_z = [exchange_zh(2, HALVES[0], dh_x[0])]
     lax.fori_loop(4, 8, double, 0)
     inv_v[...] = inv_v[...] / diag_row
+    dh_z.append(exchange_zh(2, HALVES[1], dh_x[1]))
     land(pj_core)
     coef_v[...] = jnp.dot(pj_all[...], inv_v[...], precision=HI, preferred_element_type=F32)
     land(tok_core)
@@ -318,7 +319,6 @@
                 )
             else:
                 p_own[u, :, COLS[0]] = value
-    dh_z.append(exchange_zh(2, HALVES[1], dh_x[1]))
     pre_scatter(1)
     pre_exchange(0)
     pre_scatter(2)
@@ -399,12 +399,12 @@
         rows = pl.ds(pl.multiple_of((y * 4 + zl) * n, n), n)
         return own[rows, :] + got[0].astype(F32) + got[1].astype(F32) + got[2].astype(F32)
 
-    dc_cs[...] = dc_block(half_other)
+    dc_cs[...] = dc_block(half_other).astype(BF)
     dc_c = send(dc_cs, dc_cr, to_core())
     dc_own[...] = dc_block(half_own)
     dc_c.wait_recv()
-    dc_own[...] = dc_own[...] + dc_cr[...]
-    dc_y = scatter_y(dc_own, dc_ys, dc_yr, TB, F32)
+    dc_own[...] = dc_own[...] + dc_cr[...].astype(F32)
+    dc_y = scatter_y(dc_own, dc_ys, dc_yr, TB, BF)
 
     q_part(last)
 
@@ -418,7 +418,7 @@
     g_c = send(g_cs, g_cr, to_core())
 
     after_y(dc_own, dc_yr, dc_y, TB)
-    dc_z = scatter_zl(dc_own, dc_zs, dc_zr, TB, F32)
+    dc_z = scatter_zl(dc_own, dc_zs, dc_zr, TB, BF)
 
     g_own[...] = g_block(g_half_own)
     g_c.wait_recv()
@@ -446,9 +446,10 @@
 
     dc_h.wait_recv()
     d_coeffs = -(dc_hs[...] + dc_hr[...])
-    dp_all[rows_own(TB), :] = lax.dot_general(
+    d_proj = lax.dot_general(
         d_coeffs, inv_v[...], (((1,), (1,)), ((), ())), precision=HI, preferred_element_type=F32
     )
+    dp_all[rows_own(TB), :] = d_proj.astype(BF)
     dp_zl = gather_zl(dp_all, TB)
 
     g_all[rows_own(DO), :] = after_zl(g_own, g_zr, g_z, DO).astype(BF)
@@ -468,12 +469,12 @@
     mixed_ref[...] = after_zl(mx_own, mx_zr, mx_z, TB).astype(BF)
     land(dp_core)
 
-    d_coupling = -jnp.dot(coef_t[...], dp_all[...], precision=HI, preferred_element_type=F32)
+    c_hi, c_lo = split(coef_t[...])
+    d_coupling = -(nn(c_hi, dp_all[...]) + nn(c_lo, dp_all[...]))
     sym = jnp.where(col >= row, d_coupling, jnp.transpose(d_coupling))
-    d_hi, d_lo = split(dp_all[...])
     land(g_y2)
     g_core = gather_core(g_all, DO)
-    total = nn(tok_t[...], d_hi) + nn(tok_t[...], d_lo)
+    total = nn(tok_t[...], dp_all[...])
     total = total + jnp.dot(refl_v[...], sym, precision=HI, preferred_element_type=F32)
     land(g_core)
     grad_ref[...] = total + g_all[...].astype(F32)
@@ -495,9 +496,9 @@
         v((3, TOKENS, FB), BF), v((TOKENS, R), F32), v((2, R, FB), BF), v((2, R, FB), BF),
         v((256, DB), BF), v((256, DB), BF), v((256, DB), F32),
         v((3, 64, DB), BF), v((3, 64, DB), BF), v((3, TB, DB), BF), v((3, TB, DB), BF),
-        v((256, R), F32), v((256, R), F32), v((256, R), F32),
-        v((3, 64, R), F32), v((3, 64, R), F32), v((3, TB, R), F32), v((3, TB, R), F32),
-        v((TB, R), F32), v((3, TB, R), F32), v((TB, R), F32), v((TB, R), F32), v((TOKENS, R), F32),
+        v((256, R), BF), v((256, R), BF), v((256, R), F32),
+        v((3, 64, R), BF), v((3, 64, R), BF), v((3, TB, R), BF), v((3, TB, R), BF),
+        v((TB, R), F32), v((3, TB, R), F32), v((TB, R), F32), v((TB, R), F32), v((TOKENS, R), BF),
         v((512, R), BF), v((512, R), BF), v((512, R), F32),
         v((3, 4 * DO, R), BF), v((3, 4 * DO, R), BF), v((3, DO, R), BF), v((3, DO, R), BF), v((DB, R), BF),
         dma((6,)), dma((SEMS,)), dma((SEMS,)),

time: 123 us -> 120 us (0.976)
  Pallas kernels: 119 us -> 116 us
    pallas_call x1, Pallas kernels: 119 us -> 116 us  [body(): pl.pallas_call(kernel, out_shape=(jax.ShapeDtypeStruct((TB, DB), BF), jax...]
where the time goes in v4:
time: 120 us
  Pallas kernels  116 us (97%)
  local copies, waits for them, and re-layouts  3.1 us (3%)
    pallas_call x1, Pallas kernels, body(): pl.pallas_call(kernel, out_shape=(jax.ShapeDtypeStruct((TB, DB), BF), jax...  116 us
    unnamed x6, local copies, waits for them, and re-layouts  3.1 us

profile of v4, /device:TPU:1, one launch (start us, length us, event | category | flops | bytes accessed | tf_op | source)
XLA Modules:
  0.0 120.2 jit_solution(7051053111380443659)
XLA Ops:
  0.6 0.0 copy-start
  0.6 0.7 copy-done
  1.4 0.0 copy-start.1
  1.4 0.8 copy-done.1
  2.1 116.5 %shard_map.77 = (bf16[16,1024]{1,0:T(8,128)(2,1)S(1)}, f32[1024,256]{1,0:T(8,128)S(1)}) custom-call(bf16[16,1024]{1,0:T(8,128)(2,1)S(1)} %copy-done, f32[1024,256]{1,0:T(8,128)} %refl_hbm.1, bf16[1024,896]{1,0:T(8,128)(2,1)} %gate_hbm.1, bf16[1024,896]{1,0:T(8,128)(2,1)} %up_hbm.1, bf16[896,1024]{1,0:T(8,128)(2,1)} %down_hbm.1, bf16[16,1024]{1,0:T(8,128)(2,1)S(1)} %copy-done.1), custom_call_target="tpu_custom_call" | custom-call | tf_op jit(solution)/shard_map/pallas_call | solution.py:511
  118.7 0.6 copy.10
  119.3 1.0 copy.11
Async XLA Ops:
  0.6 0.8 copy-start
  1.4 0.8 copy-start.1
